TPU v7x, 512 devices: a whole 4x8x8 slice. The times are simulated.
512 devices in a mesh: dp: 32 (over y, x), tensor: 16 (over z, core).
Axes of the slice: x: 4, y: 8, z: 8, core: 2. Of those that a mesh axis runs over, the one named last changes fastest.
Arguments:
- hidden_in: bfloat16 [2048, 12288], P('dp'), may hold values from -6 to 6
- norm_gain: bfloat16 [12288], replicated, may hold values from 0.099609375 to 1.8984375
- norm_shift: bfloat16 [12288], replicated, may hold values from -3 to 3
- up_weight: bfloat16 [12288, 24576], P('dp', 'tensor'), may hold values from -0.0546875 to 0.0546875
- up_bias: bfloat16 [24576], P('tensor'), may hold values from -3 to 3
- down_weight: bfloat16 [24576, 12288], P('tensor', 'dp'), may hold values from -0.09375 to 0.09375
- down_bias: bfloat16 [12288], P('tensor'), may hold values from -3 to 3
- active: int32 [64, 16, 4], P(None, 'tensor'), may hold values from 0 to 11, as said below
- counts: int32 [64, 16], P(None, 'tensor'), may hold values from 1 to 4, as said below
Outputs:
- hidden_out: bfloat16 [2048, 12288], P('dp', 'tensor')
Inputs may be any that keep to these rules, and one draw needn't show every extreme that they name: The 4 entries of each list are distinct; only the first counts entries are active. `counts`: every row group has a list with all 4 slots valid.
All inputs are finite; a program needn't handle non-finite values.
Results may differ from a plain program's by a relative error of at most 0.022.
Values may be sent and summed in bfloat16 or wider, within the bound.
No kernel may reach another device: no remote copies, remote signals or barrier semaphores. Data moves between devices by JAX's collectives and lax.ppermute only.
A program may use at most 64 MiB of HBM per device.

v0:
```python
import math
import jax
import jax.numpy as jnp
from jax import lax
from jax.sharding import PartitionSpec as P

BLOCK = 128
GROUP = 32


def in_blocks(step_fn, arrays):
    total = arrays[0].shape[0]
    per = math.gcd(total, 8)
    stacked = tuple((item.reshape((total // per, per) + item.shape[1:]) for item in arrays))
    result = lax.map(step_fn, stacked)
    return result.reshape((total,) + result.shape[2:])


def select_up(rows, ids, up_table):
    ngroups, slots = ids.shape
    grouped = rows.reshape(ngroups, -1, rows.shape[1])

    def step(pair):
        block_rows, block_ids = pair
        chosen = jnp.take(up_table, block_ids, axis=1)
        return jnp.einsum("grd,dgcb->grcb", block_rows, chosen, preferred_element_type=jnp.float32)

    result = in_blocks(step, (grouped, ids))
    return result.reshape(rows.shape[0], slots * up_table.shape[2])


def select_down(act, ids, down_table):
    ngroups, slots = ids.shape
    grouped = act.reshape(ngroups, -1, slots, down_table.shape[1])

    def step(pair):
        block_act, block_ids = pair
        chosen = jnp.take(down_table, block_ids, axis=0)
        return jnp.einsum("grcb,gcbd->grd", block_act, chosen, preferred_element_type=jnp.float32)

    result = in_blocks(step, (grouped, ids))
    return result.reshape(act.shape[0], down_table.shape[2])


def activate(pre, ids, valid, bias_table):
    ngroups, slots = ids.shape
    own = bias_table.shape[0]
    onehot = (ids[:, :, None] == jnp.arange(own, dtype=jnp.int32)[None, None, :]).astype(
        jnp.float32
    )
    bias_sel = jnp.einsum("gco,ob->gcb", onehot, bias_table, precision=lax.Precision.HIGHEST)
    mask = (jnp.arange(slots, dtype=jnp.int32)[None, :] < valid[:, None]).astype(jnp.float32)
    shaped = pre.reshape(ngroups, -1, slots, bias_table.shape[1])
    result = jnp.maximum(shaped + bias_sel[:, None], 0.0) * mask[:, None, :, None]
    return result.astype(jnp.bfloat16).reshape(pre.shape)


def body(
    hidden_in, norm_gain, norm_shift, up_weight, up_bias, down_weight, down_bias, active, counts
):
    row_dev = hidden_in.shape[0]
    values = hidden_in.astype(jnp.float32)
    center = values - jnp.mean(values, axis=-1, keepdims=True)
    spread = jnp.mean(center * center, axis=-1, keepdims=True)
    normed = (
        center * lax.rsqrt(spread + 1e-05) * norm_gain.astype(jnp.float32)
        + norm_shift.astype(jnp.float32)
    ).astype(jnp.bfloat16)
    columns = lax.all_to_all(normed, "dp", split_axis=1, concat_axis=0, tiled=True)
    d_part = up_weight.shape[0]
    own = up_weight.shape[1] // BLOCK
    up_table = up_weight.reshape(d_part, own, BLOCK)
    down_table = down_weight.reshape(own, BLOCK, d_part)
    bias_table = up_bias.astype(jnp.float32).reshape(own, BLOCK)
    ids = active[:, 0, :]
    valid = counts[:, 0]
    pre_own = lax.psum_scatter(
        select_up(columns, ids, up_table).astype(jnp.bfloat16),
        "dp",
        scatter_dimension=0,
        tiled=True,
    ).astype(jnp.float32)
    per_dev = row_dev // GROUP
    first = lax.axis_index("dp") * per_dev
    own_ids = lax.dynamic_slice_in_dim(ids, first, per_dev, 0)
    own_valid = lax.dynamic_slice_in_dim(valid, first, per_dev, 0)
    act_own = activate(pre_own, own_ids, own_valid, bias_table)
    act = lax.all_gather(act_own, "dp", axis=0, tiled=True)
    branch = select_down(act, ids, down_table)
    branch = branch.astype(jnp.bfloat16)
    returned = lax.all_to_all(branch, "dp", split_axis=0, concat_axis=1, tiled=True)
    summed = lax.psum_scatter(
        returned.astype(jnp.float32).astype(jnp.bfloat16), "tensor", scatter_dimension=1, tiled=True
    ).astype(jnp.float32)
    width = summed.shape[1]
    resid = lax.dynamic_slice_in_dim(hidden_in, lax.axis_index("tensor") * width, width, 1).astype(
        jnp.float32
    )
    return (resid + summed + down_bias.astype(jnp.float32)).astype(jnp.bfloat16)


def solution(mesh):
    placed = (
        P("dp", None),
        P(),
        P(),
        P("dp", "tensor"),
        P("tensor"),
        P("tensor", "dp"),
        P("tensor"),
        P(None, "tensor", None),
        P(None, "tensor"),
    )
    return jax.shard_map(
        body, mesh=mesh, in_specs=placed, out_specs=P("dp", "tensor"), check_vma=False
    )
```

profile of v0, /device:TPU:6, one launch (start us, length us, event | category | flops | bytes accessed | tf_op | source)
XLA Modules:
  0.0 595.1 jit_solution(5143126974400507887)
XLA Ops:
  6.5 1.8 convert_reduce_fusion
  9.8 1.4 copy.71
  11.2 10.4 %all-to-all-start = ((bf16[64,32,384]{2,0,1:T(8,128)(2,1)}), bf16[64,32,384]{2,0,1:T(8,128)(2,1)}, u32[]{:S(2)}, u32[]{:S(2)}) async-start(bf16[64,32,384]{2,0,1:T(8,128)(2,1)} %bitcast.85), calls=%async_computation | async-start | bytes 3145728 | tf_op jit(solution)/shard_map/all_to_all | solution.py:69
  23.2 1.7 copy.50
  24.9 36.1 %all-to-all-done = bf16[64,32,384]{2,0,1:T(8,128)(2,1)} async-done(((bf16[64,32,384]{2,0,1:T(8,128)(2,1)}), bf16[64,32,384]{2,0,1:T(8,128)(2,1)}, u32[]{:S(2)}, u32[]{:S(2)}) %all-to-all-start) | async-done | bytes 1572896 | tf_op jit(solution)/shard_map/all_to_all | solution.py:69
  60.9 51.3 %while.20 = (s32[]{:T(128)}, bf16[8,8,32,4,128]{4,2,3,1,0:T(8,128)(2,1)}, bf16[8,8,32,384]{3,2,1,0:T(8,128)(2,1)}, s32[8,8,4]{1,2,0:T(4,128)S(1)}, bf16[384,12,128]{2,0,1:T(8,128)(2,1)S(1)}, /*index=5*/s32[]{:T(128)}) while((s32[]{:T(128)}, bf16[8,8,32,4,128]{4,2,3,1,0:T(8,128)(2,1)}, bf16[8,8,32,384]{3,2,1,0:T(8,128)(2,1)}, ...), condition=%wide.region_3.4_spmd, body=%wide.region_2.3_spmd.sunk | while | flops 102237472 | bytes 10164557 | solution.py:15
  61.1 2.6 gather_fusion
  63.8 3.5 fusion.45
  67.5 2.6 gather_fusion
  70.2 3.5 fusion.45
  73.9 2.6 gather_fusion
  76.6 3.6 fusion.45
  80.3 2.6 gather_fusion
  83.0 3.5 fusion.45
  86.7 2.6 gather_fusion
  89.4 3.5 fusion.45
  93.1 2.6 gather_fusion
  95.8 3.6 fusion.45
  99.6 2.6 gather_fusion
  102.3 3.5 fusion.45
  106.0 2.6 gather_fusion
  108.7 3.5 fusion.45
  112.2 2.7 copy.51
  114.9 1.7 copy.70
  117.6 219.8 %reduce-scatter.3.cloned.1.call-done = bf16[64,512]{1,0:T(8,128)(2,1)} async-done(((bf16[2048,512]{1,0:T(8,128)(2,1)}), bf16[64,512]{1,0:T(8,128)(2,1)}) %reduce-scatter.3.cloned.1.call-update) | async-done | bytes 65552 | tf_op jit(solution)/shard_map/reduce_scatter | solution.py:77
  337.5 1.5 fusion.32
  339.1 83.5 %all-gather.2.cloned.1.call-done = bf16[2048,512]{1,0:T(8,128)(2,1)} async-done(((bf16[64,512]{1,0:T(8,128)(2,1)}), bf16[2048,512]{1,0:T(8,128)(2,1)}) %all-gather.2.cloned.1.call-update) | async-done | bytes 2097168 | tf_op jit(solution)/shard_map/all_gather | solution.py:88
  422.6 4.0 reshape_reshape.9
  426.6 57.6 %while.21 = (s32[]{:T(128)}, bf16[8,8,32,384]{3,2,1,0:T(8,128)(2,1)}, bf16[8,8,32,4,128]{4,3,2,1,0:T(4,128)(2,1)}, s32[8,8,4]{1,2,0:T(4,128)S(1)}, bf16[12,128,384]{2,1,0:T(8,128)(2,1)S(1)}, /*index=5*/s32[]{:T(128)}) while((s32[]{:T(128)}, bf16[8,8,32,384]{3,2,1,0:T(8,128)(2,1)}, bf16[8,8,32,4,128]{4,3,2,1,0:T(4,128)(2,1)}, ...), condition=%wide.region_6.7_spmd, body=%wide.region_5.6_spmd.sunk | while | flops 102237472 | bytes 10622801 | solution.py:15
  426.7 2.6 gather_fusion.1
  430.5 3.3 fusion.47
  433.9 2.6 gather_fusion.1
  437.7 3.3 fusion.47
  441.2 2.6 gather_fusion.1
  444.9 3.3 fusion.47
  448.4 2.6 gather_fusion.1
  452.1 3.3 fusion.47
  455.6 2.6 gather_fusion.1
  459.3 3.2 fusion.47
  462.8 2.6 gather_fusion.1
  466.5 3.3 fusion.47
  470.0 2.6 gather_fusion.1
  473.7 3.2 fusion.47
  477.1 2.6 gather_fusion.1
  480.9 3.3 fusion.47
  484.2 42.5 %all_to_all.32 = bf16[32,64,384]{2,1,0:T(8,128)(2,1)S(1)} all-to-all(bf16[32,64,384]{2,1,0:T(8,128)(2,1)} %bitcast.117), channel_id=1, replica_groups=mesh['dp'=32,'tensor'=16] {'dp'}, dimensions={0} | all-to-all | bytes 3145728 | tf_op jit(solution)/shard_map/all_to_all | solution.py:91
  528.0 59.0 %reduce-scatter.5.cloned.1.call-done = bf16[64,768]{1,0:T(8,128)(2,1)} async-done(((bf16[64,12288]{1,0:T(8,128)(2,1)}), bf16[64,768]{1,0:T(8,128)(2,1)}) %reduce-scatter.5.cloned.1.call-update) | async-done | bytes 98320 | tf_op jit(solution)/shard_map/reduce_scatter | solution.py:92
  587.0 1.6 add_convert_fusion
  (148 shorter events, 18.3 us)
Async XLA Ops:
  6.5 110.9 %copy-start = (bf16[1536]{0:T(1024)(128)(2,1)S(1)}, bf16[1536]{0:T(1024)(128)(2,1)}, u32[]{:S(2)}) copy-start(bf16[1536]{0:T(1024)(128)(2,1)} %param.17) | copy-start | bytes 9220
  6.5 1.9 copy-start.2
  6.5 2.5 copy-start.4
  6.5 2.5 copy-start.5
  11.2 10.4 %copy-start.6 = (s32[64,1,4]{0,2,1:T(4,128)S(1)}, s32[64,1,4]{0,2,1:T(4,128)}, u32[]{:S(2)}) copy-start(s32[64,1,4]{0,2,1:T(4,128)} %param.20) | copy-start | bytes 3076
  11.2 10.5 %copy-start.3 = (bf16[384,1536]{1,0:T(8,128)(2,1)S(1)}, bf16[384,1536]{1,0:T(8,128)(2,1)}, u32[]{:S(2)}) copy-start(bf16[384,1536]{1,0:T(8,128)(2,1)} %param.16) | copy-start | bytes 3538948
  11.2 49.7 %all-to-all-start = ((bf16[64,32,384]{2,0,1:T(8,128)(2,1)}), bf16[64,32,384]{2,0,1:T(8,128)(2,1)}, u32[]{:S(2)}, u32[]{:S(2)}) async-start(bf16[64,32,384]{2,0,1:T(8,128)(2,1)} %bitcast.85), calls=%async_computation | async-start | bytes 3145728 | tf_op jit(solution)/shard_map/all_to_all | solution.py:69
  21.6 315.8 %reduce-scatter.3.cloned.1.call-start = ((), (), s32[]{:S(2)}) async-start(), calls=%async_computation.4 | async-start | bytes 2162688 | tf_op jit(solution)/shard_map/reduce_scatter | solution.py:77
  116.6 0.7 copy-start.8
  116.6 306.0 %all-gather.2.cloned.1.call-start = ((), (), s32[]{:S(2)}) async-start(), calls=%async_computation.5 | async-start | bytes 2162688 | tf_op jit(solution)/shard_map/all_gather | solution.py:88
  339.0 248.0 %reduce-scatter.5.cloned.1.call-start = ((), (), s32[]{:S(2)}) async-start(), calls=%async_computation.6 | async-start | bytes 1671168 | tf_op jit(solution)/shard_map/reduce_scatter | solution.py:92
  339.1 87.5 %copy-start.1 = (bf16[1536,384]{1,0:T(8,128)(2,1)S(1)}, bf16[1536,384]{1,0:T(8,128)(2,1)}, u32[]{:S(2)}) copy-start(bf16[1536,384]{1,0:T(8,128)(2,1)} %param.18) | copy-start | bytes 3538948
  526.7 1.4 copy-start.7
Sparse Core Ops, SparseCore 0:
  116.7 220.6 reduce-scatter.2
  341.0 81.5 all-gather.1
  528.1 58.8 reduce-scatter.4
where the time goes:
time: 596 us; the launch traced here: 595 us
  waiting for transfers between devices  398 us (67%)
  local copies, waits for them, and re-layouts  69.3 us (12%)
  matrix products  54.5 us (9%)
  blocking collectives  42.5 us (7%)
  between operations  13.3 us (2%)
  starting transfers between devices  10.5 us (2%)
  other arithmetic  6.56 us (1%)
    reduce_scatter x1, waiting for transfers between devices, body(): lax.psum_scatter(select_up(columns, ids, up_table).astype(jnp.bfloat16),...  220 us
    all_gather x1, waiting for transfers between devices, body(): act = lax.all_gather(act_own, 'dp', axis=0, tiled=True)  83.5 us
    reduce_scatter x1, waiting for transfers between devices, body(): lax.psum_scatter(returned.astype(jnp.float32).astype(jnp.bfloat16), 'tens...  59 us
    all_to_all x1, blocking collectives, body(): lax.all_to_all(branch, 'dp', split_axis=0, concat_axis=1, tiled=True)  42.5 us
    all_to_all x1, waiting for transfers between devices, body(): lax.all_to_all(normed, 'dp', split_axis=1, concat_axis=0, tiled=True)  36.1 us
    dot_general x8, matrix products, step(): jnp.einsum('grd,dgcb->grcb', block_rows, chosen, preferred_element_type=j...  28.3 us
    dot_general x8, matrix products, step(): jnp.einsum('grcb,gcbd->grd', block_act, chosen, preferred_element_type=jn...  26 us
    gather x8, local copies, waits for them, and re-layouts, step(): chosen = jnp.take(down_table, block_ids, axis=0)  20.9 us
  transfers between devices with their start and end apart: 4, of which 4 were waited for; matrix products, arithmetic and copies ran while one was open for 1% of the time, Pallas kernels for 0%

commit v1 on v0

--- a/solution.py
+++ b/solution.py
@@ -85,7 +85,9 @@
     own_ids = lax.dynamic_slice_in_dim(ids, first, per_dev, 0)
     own_valid = lax.dynamic_slice_in_dim(valid, first, per_dev, 0)
     act_own = activate(pre_own, own_ids, own_valid, bias_table)
-    act = lax.all_gather(act_own, "dp", axis=0, tiled=True)
+    act = jnp.concatenate(
+        lax.all_to_all(jnp.stack([act_own] * lax.axis_size("dp")), "dp", 0, 0), axis=0
+    )
     branch = select_down(act, ids, down_table)
     branch = branch.astype(jnp.bfloat16)
     returned = lax.all_to_all(branch, "dp", split_axis=0, concat_axis=1, tiled=True)

time: 596 us -> 566 us (0.950)
  waiting for transfers between devices: 398 us -> 359 us
  starting transfers between devices: 10.5 us -> 18.7 us
    all_gather x1 -> x0, waiting for transfers between devices: 83.5 us -> none  [body(): act = lax.all_gather(act_own, 'dp', axis=0, tiled=True)]
    all_to_all x0 -> x1, waiting for transfers between devices: none -> 44.6 us  [body(): lax.all_to_all(jnp.stack([act_own] * lax.axis_size('dp')), 'dp', 0, 0)]
    all_to_all x0 -> x1, starting transfers between devices: none -> 8.22 us  [body(): lax.all_to_all(jnp.stack([act_own] * lax.axis_size('dp')), 'dp', 0, 0)]
where the time goes in v1:
time: 566 us; the launch traced here: 565 us
  waiting for transfers between devices  359 us (63%)
  local copies, waits for them, and re-layouts  71 us (13%)
  matrix products  54.4 us (10%)
  blocking collectives  41.9 us (7%)
  starting transfers between devices  18.7 us (3%)
  between operations  13.6 us (2%)
  other arithmetic  5.93 us (1%)
    reduce_scatter x1, waiting for transfers between devices, body(): lax.psum_scatter(select_up(columns, ids, up_table).astype(jnp.bfloat16),...  220 us
    reduce_scatter x1, waiting for transfers between devices, body(): lax.psum_scatter(returned.astype(jnp.float32).astype(jnp.bfloat16), 'tens...  58.7 us
    all_to_all x1, waiting for transfers between devices, body(): lax.all_to_all(jnp.stack([act_own] * lax.axis_size('dp')), 'dp', 0, 0)  44.6 us
    all_to_all x1, blocking collectives, body(): lax.all_to_all(branch, 'dp', split_axis=0, concat_axis=1, tiled=True)  41.9 us
    all_to_all x1, waiting for transfers between devices, body(): lax.all_to_all(normed, 'dp', split_axis=1, concat_axis=0, tiled=True)  36.1 us
    dot_general x8, matrix products, step(): jnp.einsum('grd,dgcb->grcb', block_rows, chosen, preferred_element_type=j...  28.3 us
    dot_general x8, matrix products, step(): jnp.einsum('grcb,gcbd->grd', block_act, chosen, preferred_element_type=jn...  26 us
    gather x8, local copies, waits for them, and re-layouts, step(): chosen = jnp.take(down_table, block_ids, axis=0)  21 us
  transfers between devices with their start and end apart: 4, of which 4 were waited for; matrix products, arithmetic and copies ran while one was open for 1% of the time, Pallas kernels for 0%

profile of v1, /device:TPU:6, one launch (start us, length us, event | category | flops | bytes accessed | tf_op | source)
XLA Modules:
  0.0 564.8 jit_solution(16889448706743001342)
XLA Ops:
  6.5 1.8 convert_reduce_fusion
  11.2 10.4 %all-to-all-start = ((bf16[64,32,384]{2,0,1:T(8,128)(2,1)}), bf16[64,32,384]{2,0,1:T(8,128)(2,1)}, u32[]{:S(2)}, u32[]{:S(2)}) async-start(bf16[64,32,384]{2,0,1:T(8,128)(2,1)} %bitcast.85), calls=%async_computation | async-start | bytes 3145728 | tf_op jit(solution)/shard_map/all_to_all | solution.py:69
  23.2 1.7 copy.50
  24.9 36.1 %all-to-all-done = bf16[64,32,384]{2,0,1:T(8,128)(2,1)} async-done(((bf16[64,32,384]{2,0,1:T(8,128)(2,1)}), bf16[64,32,384]{2,0,1:T(8,128)(2,1)}, u32[]{:S(2)}, u32[]{:S(2)}) %all-to-all-start) | async-done | bytes 1572896 | tf_op jit(solution)/shard_map/all_to_all | solution.py:69
  60.9 51.3 %while.20 = (s32[]{:T(128)}, bf16[8,8,32,4,128]{4,2,3,1,0:T(8,128)(2,1)}, bf16[8,8,32,384]{3,2,1,0:T(8,128)(2,1)}, s32[8,8,4]{1,2,0:T(4,128)S(1)}, bf16[384,12,128]{2,0,1:T(8,128)(2,1)S(1)}, /*index=5*/s32[]{:T(128)}) while((s32[]{:T(128)}, bf16[8,8,32,4,128]{4,2,3,1,0:T(8,128)(2,1)}, bf16[8,8,32,384]{3,2,1,0:T(8,128)(2,1)}, ...), condition=%wide.region_3.4_spmd, body=%wide.region_2.3_spmd.sunk | while | flops 102237472 | bytes 10164557 | solution.py:15
  61.1 2.6 gather_fusion
  63.8 3.5 fusion.45
  67.5 2.6 gather_fusion
  70.2 3.5 fusion.45
  73.9 2.6 gather_fusion
  76.6 3.5 fusion.45
  80.3 2.6 gather_fusion
  83.0 3.5 fusion.45
  86.7 2.6 gather_fusion
  89.4 3.5 fusion.45
  93.1 2.6 gather_fusion
  95.8 3.6 fusion.45
  99.6 2.6 gather_fusion
  102.3 3.5 fusion.45
  106.0 2.6 gather_fusion
  108.7 3.5 fusion.45
  112.2 2.7 copy.51
  114.9 1.7 copy.70
  117.6 219.8 %reduce-scatter.3.cloned.1.call-done = bf16[64,512]{1,0:T(8,128)(2,1)} async-done(((bf16[2048,512]{1,0:T(8,128)(2,1)}), bf16[64,512]{1,0:T(8,128)(2,1)}) %reduce-scatter.3.cloned.1.call-update) | async-done | bytes 65552 | tf_op jit(solution)/shard_map/reduce_scatter | solution.py:77
  338.3 1.6 stack.3
  339.9 8.2 %all-to-all-start.1 = ((bf16[32,64,512]{2,1,0:T(8,128)(2,1)}), bf16[32,64,512]{2,1,0:T(8,128)(2,1)}, u32[]{:S(2)}, u32[]{:S(2)}) async-start(bf16[32,64,512]{2,1,0:T(8,128)(2,1)} %stack.3), calls=%async_computation.2 | async-start | bytes 4194304 | tf_op jit(solution)/shard_map/all_to_all | solution.py:89
  348.2 44.6 %all-to-all-done.1 = bf16[32,64,512]{2,1,0:T(8,128)(2,1)} async-done(((bf16[32,64,512]{2,1,0:T(8,128)(2,1)}), bf16[32,64,512]{2,1,0:T(8,128)(2,1)}, u32[]{:S(2)}, u32[]{:S(2)}) %all-to-all-start.1) | async-done | bytes 2097184 | tf_op jit(solution)/shard_map/all_to_all | solution.py:89
  392.8 4.0 reshape_reshape_reshape.3
  396.8 57.6 %while.21 = (s32[]{:T(128)}, bf16[8,8,32,384]{3,2,1,0:T(8,128)(2,1)}, bf16[8,8,32,4,128]{4,3,2,1,0:T(4,128)(2,1)}, s32[8,8,4]{1,2,0:T(4,128)S(1)}, bf16[12,128,384]{2,1,0:T(8,128)(2,1)S(1)}, /*index=5*/s32[]{:T(128)}) while((s32[]{:T(128)}, bf16[8,8,32,384]{3,2,1,0:T(8,128)(2,1)}, bf16[8,8,32,4,128]{4,3,2,1,0:T(4,128)(2,1)}, ...), condition=%wide.region_6.7_spmd, body=%wide.region_5.6_spmd.sunk | while | flops 102237472 | bytes 10622801 | solution.py:15
  397.0 2.6 gather_fusion.1
  400.7 3.2 fusion.47
  404.2 2.6 gather_fusion.1
  407.9 3.3 fusion.47
  411.4 2.6 gather_fusion.1
  415.2 3.3 fusion.47
  418.6 2.6 gather_fusion.1
  422.4 3.2 fusion.47
  425.8 2.6 gather_fusion.1
  429.6 3.2 fusion.47
  433.0 2.6 gather_fusion.1
  436.8 3.3 fusion.47
  440.2 2.6 gather_fusion.1
  444.0 3.2 fusion.47
  447.4 2.6 gather_fusion.1
  451.2 3.2 fusion.47
  454.4 41.9 %all_to_all.37 = bf16[32,64,384]{2,1,0:T(8,128)(2,1)S(1)} all-to-all(bf16[32,64,384]{2,1,0:T(8,128)(2,1)} %bitcast.117), channel_id=1, replica_groups=mesh['dp'=32,'tensor'=16] {'dp'}, dimensions={0} | all-to-all | bytes 3145728 | tf_op jit(solution)/shard_map/all_to_all | solution.py:93
  497.7 58.7 %reduce-scatter.5.cloned.1.call-done = bf16[64,768]{1,0:T(8,128)(2,1)} async-done(((bf16[64,12288]{1,0:T(8,128)(2,1)}), bf16[64,768]{1,0:T(8,128)(2,1)}) %reduce-scatter.5.cloned.1.call-update) | async-done | bytes 98320 | tf_op jit(solution)/shard_map/reduce_scatter | solution.py:94
  556.4 1.6 add_convert_fusion
  (148 shorter events, 20.5 us)
Async XLA Ops:
  6.5 110.9 %copy-start = (bf16[1536]{0:T(1024)(128)(2,1)S(1)}, bf16[1536]{0:T(1024)(128)(2,1)}, u32[]{:S(2)}) copy-start(bf16[1536]{0:T(1024)(128)(2,1)} %param.17) | copy-start | bytes 9220
  6.5 1.9 copy-start.2
  6.5 2.5 copy-start.4
  6.5 2.5 copy-start.5
  11.2 10.4 %copy-start.6 = (s32[64,1,4]{0,2,1:T(4,128)S(1)}, s32[64,1,4]{0,2,1:T(4,128)}, u32[]{:S(2)}) copy-start(s32[64,1,4]{0,2,1:T(4,128)} %param.20) | copy-start | bytes 3076
  11.2 10.5 %copy-start.3 = (bf16[384,1536]{1,0:T(8,128)(2,1)S(1)}, bf16[384,1536]{1,0:T(8,128)(2,1)}, u32[]{:S(2)}) copy-start(bf16[384,1536]{1,0:T(8,128)(2,1)} %param.16) | copy-start | bytes 3538948
  11.2 49.7 %all-to-all-start = ((bf16[64,32,384]{2,0,1:T(8,128)(2,1)}), bf16[64,32,384]{2,0,1:T(8,128)(2,1)}, u32[]{:S(2)}, u32[]{:S(2)}) async-start(bf16[64,32,384]{2,0,1:T(8,128)(2,1)} %bitcast.85), calls=%async_computation | async-start | bytes 3145728 | tf_op jit(solution)/shard_map/all_to_all | solution.py:69
  21.6 315.8 %reduce-scatter.3.cloned.1.call-start = ((), (), s32[]{:S(2)}) async-start(), calls=%async_computation.5 | async-start | bytes 2162688 | tf_op jit(solution)/shard_map/reduce_scatter | solution.py:77
  116.6 0.7 copy-start.8
  339.9 52.9 %all-to-all-start.1 = ((bf16[32,64,512]{2,1,0:T(8,128)(2,1)}), bf16[32,64,512]{2,1,0:T(8,128)(2,1)}, u32[]{:S(2)}, u32[]{:S(2)}) async-start(bf16[32,64,512]{2,1,0:T(8,128)(2,1)} %stack.3), calls=%async_computation.2 | async-start | bytes 4194304 | tf_op jit(solution)/shard_map/all_to_all | solution.py:89
  348.1 208.3 %reduce-scatter.5.cloned.1.call-start = ((), (), s32[]{:S(2)}) async-start(), calls=%async_computation.6 | async-start | bytes 1671168 | tf_op jit(solution)/shard_map/reduce_scatter | solution.py:94
  348.2 48.6 %copy-start.1 = (bf16[1536,384]{1,0:T(8,128)(2,1)S(1)}, bf16[1536,384]{1,0:T(8,128)(2,1)}, u32[]{:S(2)}) copy-start(bf16[1536,384]{1,0:T(8,128)(2,1)} %param.18) | copy-start | bytes 3538948
  496.3 1.4 copy-start.7
Sparse Core Ops, SparseCore 0:
  116.7 220.5 reduce-scatter.2
  497.8 58.5 reduce-scatter.4
